TPU v7x, 256 devices: a whole 4x4x8 slice. The times are simulated.
256 devices in a mesh: win: 4 (over z_hi, core), hap: 64 (over x, z_lo, y).
Axes of the slice: x: 4, y: 4, z: 8 (z_hi: 2, z_lo: 4; z = z_hi * 4 + z_lo), core: 2. Of those that a mesh axis runs over, the one named last changes fastest.
Arguments:
- queries: bfloat16 [24576, 512], P(('win', 'hap')), parts along dimension 0, may hold values from -6 to 6
- ref_keys: bfloat16 [65536, 512], P(('win', 'hap')), parts along dimension 0, may hold values from -6 to 6
- ref_values: bfloat16 [65536, 512], P(('win', 'hap')), parts along dimension 0, may hold values from -6 to 6
- attn_out: bfloat16 [24576, 512], P(('win', 'hap')), parts along dimension 0, may hold values from -6 to 6
- log_norm: float32 [8, 24576], P(None, ('win', 'hap')), parts along dimension 1, as said below
- w_out: bfloat16 [2048, 256], P('win'), parts along dimension 0, may hold values from -0.25 to 0.25
- dosage_truth: float32 [24576, 256], P(('win', 'hap')), parts along dimension 0, may hold values from -6 to 6
- marker_mask: int32 [1024], P('win'), parts along dimension 0, may hold values 0 or 1
Outputs:
- grad_query: bfloat16 [24576, 512], P(('win', 'hap')), parts along dimension 0
- grad_keys: float32 [65536, 512], P(('win', 'hap')), parts along dimension 0
- grad_values: float32 [65536, 512], P(('win', 'hap')), parts along dimension 0
There are 4 independent parts, one for each index of `win`. A program takes and returns all parts, laid end to end along the dimension named above; each array names one. Nothing has to cross between parts.
Inputs may be any that keep to these rules, and one draw needn't show every extreme that they name: `log_norm`: each entry lies within one unit of ln(16384) + 0.5.
All inputs are finite; a program needn't handle non-finite values.
Results may differ from a plain program's by a relative error of at most 0.019.
Values may be sent and summed in bfloat16 or wider, within the bound.
No kernel may reach another device: no remote copies, remote signals or barrier semaphores. Data moves between devices by JAX's collectives and lax.ppermute only.
A program may use at most 320 MiB of HBM per device.

v0:
```python
import jax
import jax.numpy as jnp
from jax import lax
from jax.sharding import PartitionSpec as P


def slopes(query_heads, grad_heads, norm_rows, delta_rows, key_heads, value_heads, scale):
    scores = (
        jnp.einsum("thd,rhd->htr", query_heads, key_heads, preferred_element_type=jnp.float32)
        * scale
    )
    probs = jnp.exp(scores - norm_rows[:, :, None])
    dprobs = jnp.einsum("thd,rhd->htr", grad_heads, value_heads, preferred_element_type=jnp.float32)
    dscores = (probs * (dprobs - delta_rows[:, :, None]) * scale).astype(jnp.bfloat16)
    return (probs, dscores)


def query_term(dscores, key_heads):
    return jnp.einsum("htr,rhd->thd", dscores, key_heads, preferred_element_type=jnp.float32)


def source_terms(probs, dscores, query_heads, grad_heads):
    probs_low = probs.astype(jnp.bfloat16)
    key_part = jnp.einsum("htr,thd->rhd", dscores, query_heads, preferred_element_type=jnp.float32)
    value_part = jnp.einsum(
        "htr,thd->rhd", probs_low, grad_heads, preferred_element_type=jnp.float32
    )
    rows_here = key_part.shape[0]
    return (key_part.reshape(rows_here, -1), value_part.reshape(rows_here, -1))


def split_stats(stat_rows, heads):
    return (jnp.transpose(stat_rows[:, :heads]), jnp.transpose(stat_rows[:, heads:]))


def body(queries, ref_keys, ref_values, attn_out, log_norm, w_out, dosage_truth, marker_mask):
    targets = queries.shape[0]
    width = queries.shape[1]
    heads = log_norm.shape[0]
    head_dim = width // heads
    scale = head_dim ** (-0.5)
    refs_here = ref_keys.shape[0]
    predicted = jnp.dot(attn_out, w_out, preferred_element_type=jnp.float32)
    residue = (marker_mask.astype(jnp.float32)[None, :] * (predicted - dosage_truth)).astype(
        jnp.bfloat16
    )
    grad_out = lax.dot_general(
        residue, w_out, (((1,), (1,)), ((), ())), preferred_element_type=jnp.float32
    ).astype(jnp.bfloat16)
    delta_rows = (
        (grad_out.astype(jnp.float32) * attn_out.astype(jnp.float32))
        .reshape(targets, heads, head_dim)
        .sum(-1)
    )
    local_keys = ref_keys.reshape(refs_here, heads, head_dim)
    local_values = ref_values.reshape(refs_here, heads, head_dim)
    stats_local = jnp.concatenate([jnp.transpose(log_norm), delta_rows], 1)
    stats_all = lax.all_gather(stats_local, "hap", axis=0, tiled=True)
    query_piece = lax.all_gather(queries, "hap", axis=0, tiled=True)
    grad_piece = lax.all_gather(grad_out, "hap", axis=0, tiled=True)
    rows_here = query_piece.shape[0]
    norm_rows, delta_part = split_stats(stats_all, heads)
    query_heads = query_piece.reshape(rows_here, heads, head_dim)
    grad_heads = grad_piece.reshape(rows_here, heads, head_dim)
    probs, dscores = slopes(
        query_heads, grad_heads, norm_rows, delta_part, local_keys, local_values, scale
    )
    term = query_term(dscores, local_keys).reshape(rows_here, width)
    query_all = term
    key_part, value_part = source_terms(probs, dscores, query_heads, grad_heads)
    query_all, grad_keys, grad_values = (query_all, key_part, value_part)
    grad_query = lax.psum_scatter(query_all, "hap", scatter_dimension=0, tiled=True).astype(
        jnp.bfloat16
    )
    return (grad_query, grad_keys, grad_values)


def solution(mesh):
    return jax.shard_map(
        body,
        mesh=mesh,
        in_specs=(
            P(("win", "hap"), None),
            P(("win", "hap"), None),
            P(("win", "hap"), None),
            P(("win", "hap"), None),
            P(None, ("win", "hap")),
            P("win", None),
            P(("win", "hap"), None),
            P("win"),
        ),
        out_specs=(P(("win", "hap"), None), P(("win", "hap"), None), P(("win", "hap"), None)),
        check_vma=False,
    )
```

profile of v0, /device:TPU:16, one launch (start us, length us, event | category | flops | bytes accessed | tf_op | source)
XLA Modules:
  0.0 1200.6 jit_solution(4344802131565947187)
XLA Ops:
  7.2 0.0 copy-start
  7.2 0.0 all-gather.4.cloned.1.call-start
  7.2 0.7 all-gather.4.cloned.1.call-update
  7.9 0.0 all-gather.6.cloned.1.call-start
  8.0 0.7 convert_element_type.24
  8.6 0.0 copy-done
  8.6 1.9 convert_multiply_fusion
  10.6 0.0 all-gather.6.cloned.1.call-update
  10.6 0.0 reduce-scatter.2.cloned.1.call-start
  10.7 1.1 copy.30
  11.7 1.1 copy.34
  12.8 0.1 copy.31
  13.0 0.7 maximum_bitcast_fusion
  13.7 183.7 %all-gather = f32[64,96,16]{1,2,0:T(8,128)S(1)} all-gather(f32[1,96,16]{1,2,0:T(8,128)S(1)} %maximum_bitcast_fusion), channel_id=1, replica_groups=mesh['win'=4,'hap'=64] {'hap'}, dimensions={0}, use_global_device_ids=true | all-gather | bytes 399360 | tf_op jit(solution)/shard_map/all_gather | solution.py:58
  197.4 0.2 copy.32
  197.6 0.3 reshape.42
  197.9 171.2 %all-gather.4.cloned.1.call-done = bf16[6144,512]{1,0:T(8,128)(2,1)} async-done(((bf16[96,512]{1,0:T(8,128)(2,1)}), bf16[6144,512]{1,0:T(8,128)(2,1)}) %all-gather.4.cloned.1.call-update) | async-done | bytes 6291472 | tf_op jit(solution)/shard_map/all_gather | solution.py:59
  369.1 8.7 copy.29
  377.8 20.5 %fusion.7 = f32[8,6144,256]{2,1,0:T(8,128)} fusion(bf16[6144,8,64]{0,2,1:T(8,128)(2,1)} %bitcast.36, bf16[256,8,64]{0,2,1:T(8,128)(2,1)S(1)} %bitcast.41), kind=kOutput, calls=%fused_computation.15 | convolution fusion | flops 1610612736 | bytes 56885248 | tf_op jit(solution)/shard_map/thd,rhd->htr/dot_general | solution.py:9
  398.2 329.2 %all-gather.6.cloned.1.call-done = bf16[6144,512]{1,0:T(8,128)(2,1)} async-done(((bf16[96,512]{1,0:T(8,128)(2,1)}), bf16[6144,512]{1,0:T(8,128)(2,1)}) %all-gather.6.cloned.1.call-update) | async-done | bytes 6291472 | tf_op jit(solution)/shard_map/all_gather | solution.py:60
  727.5 8.6 copy.33
  736.1 33.3 %multiply_convert_fusion = bf16[8,6144,256]{2,1,0:T(8,128)(2,1)} fusion(f32[8,6144,256]{2,1,0:T(8,128)} %fusion.7, f32[8,6144]{1,0:T(8,128)S(1)} %get-tuple-element.13, f32[8,6144]{1,0:T(8,128)S(1)} %get-tuple-element.12, bf16[6144,8,64]{0,2,1:T(8,128)(2,1)} %bitcast.39, bf16[256,8,64]{0,2,1:T(8,128)(2,1)S(1)} %bitcast.45), kind=kOutput, calls=%fused_computation | convolution fusion | flops 1686110208 | bytes 82444288 | tf_op jit(solution)/shard_map/thd,rhd->htr/dot_general | solution.py:13
  769.4 17.1 %fusion.8 = f32[8,6144,64]{1,2,0:T(8,128)} fusion(bf16[8,6144,256]{2,1,0:T(8,128)(2,1)} %multiply_convert_fusion, bf16[256,8,64]{0,2,1:T(8,128)(2,1)S(1)} %bitcast.42), kind=kOutput, calls=%fused_computation.16 | convolution fusion | flops 1610612736 | bytes 38010880 | tf_op jit(solution)/shard_map/htr,rhd->thd/dot_general | solution.py:19
  786.5 12.6 %copy.35 = f32[6144,512]{1,0:T(8,128)} copy(f32[6144,512]{0,1:T(8,128)} %bitcast.38) | data formatting | bytes 25165824 | tf_op jit(solution)/shard_map/reshape | solution.py:68
  799.1 0.0 reduce-scatter.2.cloned.1.call-update
  799.2 14.1 %fusion.9 = f32[8,256,64]{1,2,0:T(8,128)S(1)} fusion(bf16[6144,8,64]{0,2,1:T(8,128)(2,1)} %bitcast.37, bf16[8,6144,256]{2,1,0:T(8,128)(2,1)} %multiply_convert_fusion), kind=kOutput, calls=%fused_computation.17 | convolution fusion | flops 1610612736 | bytes 31981568 | tf_op jit(solution)/shard_map/htr,thd->rhd/dot_general | solution.py:24
  813.3 0.0 copy-start.1
  813.3 1.0 copy.36
  814.3 19.9 %fusion.1 = f32[8,64,256]{2,1,0:T(8,128)S(1)} fusion(bf16[6144,8,64]{0,2,1:T(8,128)(2,1)} %bitcast.40, f32[8,6144,256]{2,1,0:T(8,128)} %fusion.7, f32[8,6144]{1,0:T(8,128)S(1)} %get-tuple-element.12), kind=kOutput, calls=%fused_computation.3 | convolution fusion | flops 1648361472 | bytes 57344000 | tf_op jit(solution)/shard_map/htr,thd->rhd/dot_general | solution.py:25
  834.2 1.0 copy.37
  835.2 357.4 %reduce-scatter.2.cloned.1.call-done = f32[96,512]{1,0:T(8,128)} async-done(((f32[6144,512]{1,0:T(8,128)}), f32[96,512]{1,0:T(8,128)}) %reduce-scatter.2.cloned.1.call-update) | async-done | bytes 196624 | tf_op jit(solution)/shard_map/reduce_scatter | solution.py:72
  1192.5 1.6 convert_element_type.30
  1194.1 0.0 copy-done.1
  (2 shorter events, 0.1 us)
Async XLA Ops:
  7.2 1.5 copy-start
  7.2 361.9 %all-gather.4.cloned.1.call-start = ((), (), s32[]{:S(2)}) async-start(), calls=%async_computation.1 | async-start | bytes 6389760 | tf_op jit(solution)/shard_map/all_gather | solution.py:59
  7.9 719.6 %all-gather.6.cloned.1.call-start = ((), (), s32[]{:S(2)}) async-start(), calls=%async_computation.2 | async-start | bytes 6389760 | tf_op jit(solution)/shard_map/all_gather | solution.py:60
  10.6 1181.9 %reduce-scatter.2.cloned.1.call-start = ((), (), s32[]{:S(2)}) async-start(), calls=%async_computation.3 | async-start | bytes 12779520 | tf_op jit(solution)/shard_map/reduce_scatter | solution.py:72
  813.3 380.8 %copy-start.1 = (bf16[512,256]{1,0:T(8,128)(2,1)S(1)}, bf16[512,256]{1,0:T(8,128)(2,1)}, u32[]{:S(2)}) copy-start(bf16[512,256]{1,0:T(8,128)(2,1)} %param.13) | copy-start | bytes 786436
Sparse Core Ops, SparseCore 0:
  9.8 359.2 all-gather.3
  371.5 355.9 all-gather.5
  799.3 393.1 reduce-scatter.1
where the time goes:
time: 1210 us; the launch traced here: 1200 us
  waiting for transfers between devices  859 us (71%)
  blocking collectives  184 us (15%)
  matrix products  107 us (9%)
  local copies, waits for them, and re-layouts  34.7 us (3%)
  between operations  13.8 us (1%)
    reduce_scatter x1, waiting for transfers between devices, body(): lax.psum_scatter(query_all, 'hap', scatter_dimension=0, tiled=True)  357 us
    all_gather x1, waiting for transfers between devices, body(): grad_piece = lax.all_gather(grad_out, 'hap', axis=0, tiled=True)  329 us
    all_gather x1, blocking collectives, body(): stats_all = lax.all_gather(stats_local, 'hap', axis=0, tiled=True)  184 us
    all_gather x1, waiting for transfers between devices, body(): query_piece = lax.all_gather(queries, 'hap', axis=0, tiled=True)  171 us
    dot_general x1, matrix products, slopes(): jnp.einsum('thd,rhd->htr', grad_heads, value_heads, preferred_element_typ...  33.3 us
  transfers between devices with their start and end apart: 3, of which 3 were waited for; matrix products, arithmetic and copies ran while one was open for 6% of the time, Pallas kernels for 0%

commit v1 on v0

v1 whole, which is shorter than its diff:
```python
import functools

import numpy as np

import jax
import jax.numpy as jnp
from jax import lax
from jax.experimental import pallas as pl
from jax.experimental.pallas import tpu as pltpu
from jax.sharding import PartitionSpec as P

F32 = jnp.float32
BF16 = jnp.bfloat16
AXES = ("win", "hap")
NT = (((1,), (1,)), ((), ()))
NN = (((1,), (0,)), ((), ()))
TN = (((0,), (0,)), ((), ()))
HEADS = 8
HALF = 64
LANES = 128
NORM_PARTS = 3
DELTA_PARTS = 2
RANK = 4


def dot(a, b, dims):
    return lax.dot_general(a, b, dims, preferred_element_type=F32)


def exchange(array, axis, masks):
    pairs = []
    for win in range(RANK):
        mask = masks[win % 2]
        for x in range(RANK):
            for z in range(RANK):
                for y in range(RANK):
                    to = {
                        "x": (x ^ mask, z, y),
                        "z": (x, z ^ mask, y),
                        "y": (x, z, y ^ mask),
                    }[axis]
                    source = win * 64 + x * 16 + z * 4 + y
                    target = win * 64 + to[0] * 16 + to[1] * 4 + to[2]
                    pairs.append((source, target))
    return lax.ppermute(array, AXES, pairs)


X_STEPS = ((1, 3), (3, 1))
Y_STEPS = ((1, 3), (3, 1))
Z_MASKS = (1, 2, 3)
PIECE = 384
T_TILE = 256


def split_parts(value, count):
    parts = []
    for _ in range(count):
        part = value.astype(BF16)
        parts.append(part)
        value = value - part.astype(F32)
    return parts


def place_matrices():
    norm_place = np.zeros((NORM_PARTS * HEADS, LANES), np.float32)
    for row in range(NORM_PARTS * HEADS):
        norm_place[row, row] = 1
    head_sum = np.zeros((HEADS * HALF, LANES), np.float32)
    for feature in range(HEADS * HALF):
        for part in range(DELTA_PARTS):
            head_sum[feature, (NORM_PARTS + part) * HEADS + feature // HALF] = 1
    spread = np.zeros((LANES, HEADS // 2, LANES), np.float32)
    for head in range(HEADS):
        pair, odd = head // 2, head % 2
        first = 0 if odd else HALF
        for part in range(NORM_PARTS + DELTA_PARTS):
            spread[part * HEADS + head, pair, first + part] = 1
    return norm_place, head_sum, spread.reshape(LANES, HEADS // 2 * LANES)


def prologue_kernel(
    queries, attn, w_out, truth, mask, log_norm, norm_place, head_sum, keys, values,
    message, pack,
):
    pack[:, :512] = keys[...]
    pack[:, 512:] = values[...]
    attn_rows = attn[...]
    predicted = dot(attn_rows, w_out[...], NN)
    residue = (mask[...].astype(F32) * (predicted - truth[...])).astype(BF16)
    grad_out = dot(residue, w_out[...], NT).astype(BF16)
    product = grad_out.astype(F32) * attn_rows.astype(F32)
    sums = head_sum[...]
    delta = jnp.zeros((attn_rows.shape[0], LANES), F32)
    for part in split_parts(product, 3):
        delta = delta + dot(part, sums, NN)
    delta = -delta
    delta_high = delta.astype(BF16)
    delta_low = (delta - delta_high.astype(F32)).astype(BF16)
    norm_rows = jnp.concatenate(
        [part.astype(F32) for part in split_parts(-log_norm[...], NORM_PARTS)], 0
    ).astype(BF16)
    norms = dot(norm_rows, norm_place[...], TN)
    lane = lax.broadcasted_iota(jnp.int32, norms.shape, 1)
    deltas = jnp.where(
        lane < (NORM_PARTS + 1) * HEADS, delta_high.astype(F32), delta_low.astype(F32)
    )
    message[:, :512] = queries[...]
    message[:, 512:768] = residue
    message[:, 768:] = (norms + deltas).astype(BF16)


def attention_kernel(tiles, refs, carried, *args):
    count = len(tiles)
    args = list(args)
    take = lambda n: [args.pop(0) for _ in range(n)]
    q_refs, res_refs, st_refs = take(count), take(count), take(count)
    k_refs, v_refs = take(len(refs)), take(len(refs))
    w_out, spread = take(2)
    sums_in = take(2) if carried else None
    gq_outs = take(sum(tiles) // PIECE)
    g_outs = take(len(refs)) if carried else take(2)
    qs, gs, ks, vs, gk_sum, gv_sum = args
    lane = lax.broadcasted_iota(jnp.int32, (1, LANES), 1)
    low = lane < HALF
    place = lane % HALF
    one, zero = jnp.ones((), BF16), jnp.zeros((), BF16)
    norm_lanes = jnp.where(place < NORM_PARTS, one, zero)
    delta_lanes = jnp.where(
        place < NORM_PARTS, zero, jnp.where(place < NORM_PARTS + DELTA_PARTS, one, zero)
    )
    start = 0
    for size, q_ref, res_ref, st_ref in zip(tiles, q_refs, res_refs, st_refs):
        rows = slice(start, start + size)
        start += size
        grads = dot(res_ref[...], w_out[...], NT).astype(BF16)
        extra = dot(st_ref[...], spread[...], NN).astype(BF16)
        query = q_ref[...]
        qs[0, rows, :] = jnp.where(low, query, extra)
        qs[1, rows, :] = jnp.where(low, extra, query)
        gs[0, rows, :] = jnp.where(low, grads, extra)
        gs[1, rows, :] = jnp.where(low, extra, grads)
    start = 0
    for size, k_ref, v_ref in zip(refs, k_refs, v_refs):
        rows = slice(start, start + size)
        start += size
        keys = k_ref[...] * jnp.asarray(0.125, BF16)
        values = v_ref[...]
        ks[0, rows, :] = jnp.where(low, keys, norm_lanes)
        ks[1, rows, :] = jnp.where(low, norm_lanes, keys)
        vs[0, rows, :] = jnp.where(low, values, delta_lanes)
        vs[1, rows, :] = jnp.where(low, delta_lanes, values)
    for first in range(0, sum(tiles), T_TILE):
        rows = slice(first, first + T_TILE)
        gq = []
        for odd in range(2):
            query, grads, keys = qs[odd, rows, :], gs[odd, rows, :], ks[odd]
            probs = jnp.exp(dot(query, keys, NT))
            slopes = (probs * dot(grads, vs[odd], NT)).astype(BF16)
            gq.append(dot(slopes, keys, NN))
            half = slice(odd * HALF, (odd + 1) * HALF)
            key_term = dot(query, slopes, TN)[half]
            value_term = dot(grads, probs.astype(BF16), TN)[half]
            if first:
                gk_sum[half, :] += key_term
                gv_sum[half, :] += value_term
            elif carried:
                gk_sum[half, :] = sums_in[0][half, :] + key_term
                gv_sum[half, :] = sums_in[1][half, :] + value_term
            else:
                gk_sum[half, :] = key_term
                gv_sum[half, :] = value_term
        gq = jnp.where(low, gq[0], gq[1]).astype(BF16)
        at = first
        while at < first + T_TILE:
            piece = at // PIECE
            stop = min(first + T_TILE, (piece + 1) * PIECE)
            gq_outs[piece][at - piece * PIECE : stop - piece * PIECE, :] = gq[
                at - first : stop - first
            ]
            at = stop
    here = pl.multiple_of(pl.program_id(0) * LANES, LANES)
    if not carried:
        g_outs[0][...] = gk_sum[...]
        g_outs[1][...] = gv_sum[...]
        return
    start = 0
    for size, out in zip(refs, g_outs):
        cols = slice(start, start + size)
        start += size
        out[:, pl.ds(here, LANES)] = (gk_sum[:, cols].T * 0.125).astype(BF16)
        out[:, pl.ds(out.shape[1] // 2 + here, LANES)] = gv_sum[:, cols].T.astype(BF16)


def attention(messages, packs, w_out, spread, first, pairs, sums=None):
    carried = sums is not None
    tiles = tuple(m.shape[0] for m in messages)
    refs = tuple(p.shape[0] for p in packs)
    targets, total = sum(tiles), sum(refs)
    spec = pl.BlockSpec
    in_specs = [spec((t, LANES), lambda j: (0, first + j)) for t in tiles]
    in_specs += [spec((t, 256), lambda j: (0, 2)) for t in tiles]
    in_specs += [spec((t, LANES), lambda j: (0, 6)) for t in tiles]
    in_specs += [spec((r, LANES), lambda j: (0, first + j)) for r in refs]
    in_specs += [spec((r, LANES), lambda j: (0, 4 + first + j)) for r in refs]
    in_specs += [
        spec((LANES, 256), lambda j: (first + j, 0)),
        spec((LANES, LANES), lambda j: (0, first + j)),
    ]
    operands = list(messages) * 3 + list(packs) * 2 + [w_out, spread]
    out_specs = [spec((PIECE, LANES), lambda j: (0, j))] * (targets // PIECE)
    out_shape = [jax.ShapeDtypeStruct((PIECE, pairs * LANES), BF16)] * (targets // PIECE)
    if carried:
        in_specs += [spec((LANES, total), lambda j: (first + j, 0))] * 2
        operands += list(sums)
        out_specs += [spec((r, 2 * LANES * pairs), lambda j: (0, 0)) for r in refs]
        out_shape += [jax.ShapeDtypeStruct((r, 2 * LANES * pairs), BF16) for r in refs]
    else:
        out_specs += [spec((LANES, total), lambda j: (j, 0))] * 2
        out_shape += [jax.ShapeDtypeStruct((LANES * pairs, total), F32)] * 2
    return pl.pallas_call(
        functools.partial(attention_kernel, tiles, refs, carried),
        grid=(pairs,),
        in_specs=in_specs,
        out_specs=out_specs,
        out_shape=out_shape,
        scratch_shapes=[
            pltpu.VMEM((2, targets, LANES), BF16),
            pltpu.VMEM((2, targets, LANES), BF16),
            pltpu.VMEM((2, total, LANES), BF16),
            pltpu.VMEM((2, total, LANES), BF16),
            pltpu.VMEM((LANES, total), F32),
            pltpu.VMEM((LANES, total), F32),
        ],
        compiler_params=pltpu.CompilerParams(vmem_limit_bytes=62 * 2**20),
        cost_estimate=pl.CostEstimate(
            flops=40 * targets * total * pairs * LANES, bytes_accessed=2**22, transcendentals=0
        ),
    )(*operands)


def total_of(parts):
    return sum(part.astype(F32) for part in parts).astype(BF16)


def body(queries, ref_keys, ref_values, attn_out, log_norm, w_out, dosage_truth, marker_mask):
    norm_place, head_sum, spread = (jnp.asarray(m, BF16) for m in place_matrices())
    message, pack = pl.pallas_call(
        prologue_kernel,
        out_shape=[
            jax.ShapeDtypeStruct((queries.shape[0], 896), BF16),
            jax.ShapeDtypeStruct((ref_keys.shape[0], 1024), BF16),
        ],
        compiler_params=pltpu.CompilerParams(vmem_limit_bytes=62 * 2**20),
    )(
        queries, attn_out, w_out, dosage_truth, marker_mask[None, :], log_norm,
        norm_place, head_sum, ref_keys, ref_values,
    )
    pack = jnp.concatenate([pack, exchange(pack, "y", Y_STEPS[0])], 0)
    along = [exchange(message, "z", (m, m)) for m in Z_MASKS]
    pack, along[0] = lax.optimization_barrier((pack, along[0]))
    message = jnp.concatenate([message] + along, 0)
    pack_far = exchange(pack, "y", Y_STEPS[1])
    beside = exchange(message, "x", X_STEPS[0])
    both = jnp.concatenate([message, beside], 0)
    far = exchange(both, "x", X_STEPS[1])
    packs = [pack, pack_far]

    gq_mine, gq_beside, *sums = attention([both], packs, w_out, spread, 0, 4)
    back = exchange(gq_beside, "x", X_STEPS[0])
    gq_near, gq_far, near_kv, far_kv = attention([far], packs, w_out, spread, 0, 4, sums)
    back, gq_near, gq_far, far_kv = lax.optimization_barrier((back, gq_near, gq_far, far_kv))
    got_kv = exchange(far_kv, "y", Y_STEPS[1])
    across = exchange(gq_far, "x", (2, 2))
    near = exchange(gq_near, "x", X_STEPS[1])

    gq = total_of([gq_mine, back, near, across])
    half_kv = near_kv.astype(F32) + got_kv.astype(F32)
    refs_here = ref_keys.shape[0]
    other = half_kv[refs_here:].astype(BF16)
    gq, other = lax.optimization_barrier((gq, other))
    quarter = gq.shape[0] // RANK
    part = lambda at: gq[at * quarter : (at + 1) * quarter]
    grad_query = total_of(
        [part(0)]
        + [exchange(part(at + 1), "z", (m, m)) for at, m in enumerate(Z_MASKS)]
    )
    total = half_kv[:refs_here] + exchange(other, "y", Y_STEPS[0]).astype(F32)
    return grad_query, total[:, :512], total[:, 512:]


def solution(mesh):
    rows = P(("win", "hap"), None)
    return jax.shard_map(
        body,
        mesh=mesh,
        in_specs=(
            rows, rows, rows, rows,
            P(None, ("win", "hap")),
            P("win", None),
            rows,
            P("win"),
        ),
        out_specs=(rows, rows, rows),
        check_vma=False,
    )
```

time: 1210 us -> 110 us (0.09)
  waiting for transfers between devices: 859 us -> 40 us
  blocking collectives: 184 us -> 0 us
  matrix products: 107 us -> 0 us
  Pallas kernels: 0 us -> 39.4 us
  local copies, waits for them, and re-layouts: 34.7 us -> 4.81 us
  starting transfers between devices: 0.12 us -> 21.9 us
  between operations: 13.8 us -> 0.74 us
    all_gather x2 -> x0, waiting for transfers between devices: 500 us -> none  [the longest x1 329 us: body(): grad_piece = lax.all_gather(grad_out, 'hap', axis=0, tiled=True)]
    reduce_scatter x1 -> x0, waiting for transfers between devices: 357 us -> none  [body(): lax.psum_scatter(query_all, 'hap', scatter_dimension=0, tiled=True)]
    all_gather x1 -> x0, blocking collectives: 184 us -> none  [body(): stats_all = lax.all_gather(stats_local, 'hap', axis=0, tiled=True)]
    dot_general x6 -> x0, matrix products: 107 us -> none  [the longest x1 33.3 us: slopes(): jnp.einsum('thd,rhd->htr', grad_heads, value_heads, preferred_element_typ...]
    ppermute x0 -> x15, waiting for transfers between devices: none -> 40 us  [exchange(): return lax.ppermute(array, AXES, pairs)]
    pallas_call x0 -> x3, Pallas kernels: none -> 39.4 us  [the longest x2 36.7 us: attention(): pl.pallas_call(functools.partial(attention_kernel, tiles, refs, carried),...]
    ppermute x0 -> x15, starting transfers between devices: none -> 21.9 us  [exchange(): return lax.ppermute(array, AXES, pairs)]
    all_gather x3 -> x0, local copies, waits for them, and re-layouts: 17.5 us -> none  [the longest x1 8.65 us: body(): query_piece = lax.all_gather(queries, 'hap', axis=0, tiled=True)]
  transfers between devices with their start and end apart: 3 -> 15, of which waited for: 3 -> 8; matrix products, arithmetic and copies ran while one was open for 6% -> 5% of each run, Pallas kernels for 0% -> 33%
where the time goes in v1:
time: 110 us
  waiting for transfers between devices  40 us (36%)
  Pallas kernels  39.4 us (36%)
  starting transfers between devices  21.9 us (20%)
  local copies, waits for them, and re-layouts  4.81 us (4%)
  other arithmetic  2.62 us (2%)
    ppermute x15, waiting for transfers between devices, exchange(): return lax.ppermute(array, AXES, pairs)  40 us
    pallas_call x2, Pallas kernels, attention(): pl.pallas_call(functools.partial(attention_kernel, tiles, refs, carried),...  36.7 us
    ppermute x15, starting transfers between devices, exchange(): return lax.ppermute(array, AXES, pairs)  21.9 us
    pallas_call x1, Pallas kernels, body(): pl.pallas_call(prologue_kernel, out_shape=[jax.ShapeDtypeStruct((queries....  2.76 us
    unnamed x12, local copies, waits for them, and re-layouts  2.74 us
  transfers between devices with their start and end apart: 15, of which 8 were waited for; matrix products, arithmetic and copies ran while one was open for 5% of the time, Pallas kernels for 33%

profile of v1, /device:TPU:16, one launch (start us, length us, event | category | flops | bytes accessed | tf_op | source)
XLA Modules:
  0.0 109.5 jit_solution(7865264709990670231)
XLA Ops:
  0.6 2.8 %shard_map.130 = (bf16[96,896]{1,0:T(8,128)(2,1)}, bf16[256,1024]{1,0:T(8,128)(2,1)}) custom-call(bf16[96,512]{1,0:T(8,128)(2,1)} %queries.1, bf16[96,512]{1,0:T(8,128)(2,1)} %attn.1, bf16[512,256]{1,0:T(8,128)(2,1)} %args_7_.6, f32[96,256]{1,0:T(8,128)} %truth.1, s32[1,256]{1,0:T(1,128)} %bitcast.1, f32[8,96]{1,0:T(8,128)} %log_norm.1, ...), custom_call_target="tpu_custom_call" | custom-call | tf_op jit(solution)/shard_map/pallas_call | solution.py:247
  3.4 0.0 copy-start.2
  3.4 1.3 %collective-permute-start = (bf16[256,1024]{1,0:T(8,128)(2,1)}, bf16[256,1024]{1,0:T(8,128)(2,1)S(1)}, u32[]{:S(2)}, u32[]{:S(2)}) collective-permute-start(bf16[256,1024]{1,0:T(8,128)(2,1)} %get-tuple-element.22), channel_id=1, source_target_pairs={{0,1},{1,0},{2,3},{3,2},{4,5},{5,4},{6,7},{7,6},{8,9},{9,8},{10,11... | collective-permute-start | bytes 1572872 | tf_op jit(solution)/shard_map/ppermute | solution.py:45
  4.7 1.9 %collective-permute-start.1 = (bf16[96,896]{1,0:T(8,128)(2,1)}, bf16[96,896]{1,0:T(8,128)(2,1)S(1)}, u32[]{:S(2)}, u32[]{:S(2)}) collective-permute-start(bf16[96,896]{1,0:T(8,128)(2,1)} %get-tuple-element.21), channel_id=1, source_target_pairs={{0,4},{1,5},{2,6},{3,7},{4,0},{5,1},{6,2},{7,3},{8,12},{9,13},{10,... | collective-permute-start | bytes 516104 | tf_op jit(solution)/shard_map/ppermute | solution.py:45
  6.6 2.8 %collective-permute-start.3 = (bf16[96,896]{1,0:T(8,128)(2,1)}, bf16[96,896]{1,0:T(8,128)(2,1)S(1)}, u32[]{:S(2)}, u32[]{:S(2)}) collective-permute-start(bf16[96,896]{1,0:T(8,128)(2,1)} %get-tuple-element.21), channel_id=1, source_target_pairs={{0,12},{1,13},{2,14},{3,15},{4,8},{5,9},{6,10},{7,11},{8,4},{9,5},... | collective-permute-start | bytes 516104 | tf_op jit(solution)/shard_map/ppermute | solution.py:45
  9.4 0.5 collective-permute-start.2
  9.9 2.9 %collective-permute-done = bf16[256,1024]{1,0:T(8,128)(2,1)S(1)} collective-permute-done((bf16[256,1024]{1,0:T(8,128)(2,1)}, bf16[256,1024]{1,0:T(8,128)(2,1)S(1)}, u32[]{:S(2)}, u32[]{:S(2)}) %collective-permute-start) | collective-permute-done | bytes 524320 | tf_op jit(solution)/shard_map/ppermute | solution.py:45
  12.8 1.1 %pad_maximum_fusion.args_3_.args_5_ = bf16[512,1024]{1,0:T(8,128)(2,1)S(1)} fusion(bf16[256,1024]{1,0:T(8,128)(2,1)S(1)} %collective-permute-done, bf16[256,1024]{1,0:T(8,128)(2,1)} %get-tuple-element.22), kind=kLoop, calls=%fused_computation.3 | loop fusion | flops 2097152 | bytes 2097152 | tf_op jit(solution)/shard_map/concatenate | solution.py:258
  13.9 0.0 copy-start
  13.9 0.0 collective-permute-done.1
  13.9 0.7 collective-permute-start.5
  14.6 3.7 %collective-permute-done.3 = bf16[96,896]{1,0:T(8,128)(2,1)S(1)} collective-permute-done((bf16[96,896]{1,0:T(8,128)(2,1)}, bf16[96,896]{1,0:T(8,128)(2,1)S(1)}, u32[]{:S(2)}, u32[]{:S(2)}) %collective-permute-start.3) | collective-permute-done | bytes 172064 | tf_op jit(solution)/shard_map/ppermute | solution.py:45
  18.3 5.8 %collective-permute-done.2 = bf16[96,896]{1,0:T(8,128)(2,1)S(1)} collective-permute-done((bf16[96,896]{1,0:T(8,128)(2,1)}, bf16[96,896]{1,0:T(8,128)(2,1)S(1)}, u32[]{:S(2)}, u32[]{:S(2)}) %collective-permute-start.2) | collective-permute-done | bytes 172064 | tf_op jit(solution)/shard_map/ppermute | solution.py:45
  24.2 0.0 copy-done.2
  24.2 0.1 pad_maximum_fusion.1
  24.2 1.6 %collective-permute-start.4 = (bf16[384,896]{1,0:T(8,128)(2,1)S(1)}, bf16[384,896]{1,0:T(8,128)(2,1)S(1)}, u32[]{:S(2)}, u32[]{:S(2)}) collective-permute-start(bf16[384,896]{1,0:T(8,128)(2,1)S(1)} %pad_maximum_fusion.1), channel_id=1, source_target_pairs={{0,16},{1,17},{2,18},{3,19},{4,20},{5,21},{6,22},{7,23},{8,24},{9,... | collective-permute-start | bytes 2064392 | tf_op jit(solution)/shard_map/ppermute | solution.py:45
  25.8 0.7 constant_dynamic-update-slice_fusion.4
  26.5 0.7 constant_dynamic-update-slice_fusion.3
  27.2 0.7 constant_dynamic-update-slice_fusion.2
  27.9 0.7 constant_dynamic-update-slice_fusion.1
  28.5 0.0 copy-done
  28.5 6.7 %collective-permute-done.4 = bf16[384,896]{1,0:T(8,128)(2,1)S(1)} collective-permute-done((bf16[384,896]{1,0:T(8,128)(2,1)S(1)}, bf16[384,896]{1,0:T(8,128)(2,1)S(1)}, u32[]{:S(2)}, u32[]{:S(2)}) %collective-permute-start.4) | collective-permute-done | bytes 688160 | tf_op jit(solution)/shard_map/ppermute | solution.py:45
  35.2 0.9 constant_dynamic-update-slice_fusion.args_0_.args_1_.args_2_
  36.2 2.8 %collective-permute-start.7 = (bf16[768,896]{1,0:T(8,128)(2,1)}, bf16[768,896]{1,0:T(8,128)(2,1)}, u32[]{:S(2)}, u32[]{:S(2)}) collective-permute-start(bf16[768,896]{1,0:T(8,128)(2,1)} %constant_dynamic-update-slice_fusion.args_0_.args_1_.args_2_), channel_id=1, source_target_pairs={{0,48},{1,49},{2,50},{3,51},{4,52},{5,53},{6,54},{7,55},{8,56},{9,... | collective-permute-start | bytes 4128776 | tf_op jit(solution)/shard_map/ppermute | solution.py:45
  38.9 0.0 collective-permute-done.5.args_4_.args_6_
  38.9 17.6 %shard_map.131 = (bf16[384,512]{1,0:T(8,128)(2,1)}, bf16[384,512]{1,0:T(8,128)(2,1)}, f32[512,1024]{1,0:T(8,128)}, f32[512,1024]{1,0:T(8,128)}) custom-call(bf16[768,896]{1,0:T(8,128)(2,1)} %constant_dynamic-update-slice_fusion.args_0_.args_1_.args_2_, bf16[768,896]{1,0:T(8,128)(2,1)} %constant_dynamic-update-slice_fusion.args_0_.args_1_.args_2_, ...), custom_call_target="tpu_custom_call" | custom-call | flops 16106127360 | bytes 4194304 | tf_op jit(solution)/shard_map/pallas_call | solution.py:220
  56.6 0.5 collective-permute-start.6
  57.1 0.0 collective-permute-done.7.args_0_.args_1_.args_2_
  57.1 0.0 copy-start.3
  57.1 19.0 %shard_map.132 = (bf16[384,512]{1,0:T(8,128)(2,1)}, bf16[384,512]{1,0:T(8,128)(2,1)}, bf16[512,1024]{1,0:T(8,128)(2,1)}, bf16[512,1024]{1,0:T(8,128)(2,1)}) custom-call(bf16[768,896]{1,0:T(8,128)(2,1)} %collective-permute-done.7.args_0_.args_1_.args_2_, bf16[768,896]{1,0:T(8,128)(2,1)} %collective-permute-done.7.args_0_.args_1_.args_2_, ...), custom_call_target="tpu_custom_call" | custom-call | flops 16106127360 | bytes 4194304 | tf_op jit(solution)/shard_map/pallas_call | solution.py:220
  76.1 0.0 copy-start.1
  76.1 0.0 collective-permute-done.6
  76.2 1.7 %collective-permute-start.10 = (bf16[512,1024]{1,0:T(8,128)(2,1)}, bf16[512,1024]{1,0:T(8,128)(2,1)S(1)}, u32[]{:S(2)}, u32[]{:S(2)}) collective-permute-start(bf16[512,1024]{1,0:T(8,128)(2,1)} %get-tuple-element.36), channel_id=1, source_target_pairs={{0,3},{1,2},{2,1},{3,0},{4,7},{5,6},{6,5},{7,4},{8,11},{9,10},{10,... | collective-permute-start | bytes 3145736 | tf_op jit(solution)/shard_map/ppermute | solution.py:45
  77.8 1.7 %collective-permute-start.8 = (bf16[384,512]{1,0:T(8,128)(2,1)}, bf16[384,512]{1,0:T(8,128)(2,1)S(1)}, u32[]{:S(2)}, u32[]{:S(2)}) collective-permute-start(bf16[384,512]{1,0:T(8,128)(2,1)} %get-tuple-element.33), channel_id=1, source_target_pairs={{0,48},{1,49},{2,50},{3,51},{4,52},{5,53},{6,54},{7,55},{8,56},{9,... | collective-permute-start | bytes 1179656 | tf_op jit(solution)/shard_map/ppermute | solution.py:45
  79.5 2.2 %collective-permute-start.9 = (bf16[384,512]{1,0:T(8,128)(2,1)}, bf16[384,512]{1,0:T(8,128)(2,1)S(1)}, u32[]{:S(2)}, u32[]{:S(2)}) collective-permute-start(bf16[384,512]{1,0:T(8,128)(2,1)} %get-tuple-element.34), channel_id=1, source_target_pairs={{0,32},{1,33},{2,34},{3,35},{4,36},{5,37},{6,38},{7,39},{8,40},{9,... | collective-permute-start | bytes 1179656 | tf_op jit(solution)/shard_map/ppermute | solution.py:45
  81.7 13.4 %collective-permute-done.8 = bf16[384,512]{1,0:T(8,128)(2,1)S(1)} collective-permute-done((bf16[384,512]{1,0:T(8,128)(2,1)}, bf16[384,512]{1,0:T(8,128)(2,1)S(1)}, u32[]{:S(2)}, u32[]{:S(2)}) %collective-permute-start.8) | collective-permute-done | bytes 393248 | tf_op jit(solution)/shard_map/ppermute | solution.py:45
  95.0 0.0 collective-permute-done.9
  95.0 0.0 copy-done.3
  95.0 0.2 add_convert_fusion
  95.2 0.0 collective-permute-done.10
  95.2 0.0 copy-done.1
  95.3 0.4 convert_add_fusion
  95.7 0.1 slice.40
  95.7 0.8 collective-permute-start.14
  96.5 0.2 collective-permute-start.11
  96.7 2.8 %collective-permute-start.13 = (bf16[96,512]{1,0:T(8,128)(2,1)S(1)}, bf16[96,512]{1,0:T(8,128)(2,1)S(1)}, u32[]{:S(2)}, u32[]{:S(2)}) collective-permute-start(bf16[96,512]{1,0:T(8,128)(2,1)S(1)} %get-tuple-element.42), channel_id=1, source_target_pairs={{0,12},{1,13},{2,14},{3,15},{4,8},{5,9},{6,10},{7,11},{8,4},{9,5},... | collective-permute-start | bytes 294920 | tf_op jit(solution)/shard_map/ppermute | solution.py:45
  99.5 0.6 collective-permute-start.12
  100.1 2.4 %collective-permute-done.11 = bf16[96,512]{1,0:T(8,128)(2,1)S(1)} collective-permute-done((bf16[96,512]{1,0:T(8,128)(2,1)S(1)}, bf16[96,512]{1,0:T(8,128)(2,1)S(1)}, u32[]{:S(2)}, u32[]{:S(2)}) %collective-permute-start.11) | collective-permute-done | bytes 98336 | tf_op jit(solution)/shard_map/ppermute | solution.py:45
  102.5 1.7 %collective-permute-done.13 = bf16[96,512]{1,0:T(8,128)(2,1)S(1)} collective-permute-done((bf16[96,512]{1,0:T(8,128)(2,1)S(1)}, bf16[96,512]{1,0:T(8,128)(2,1)S(1)}, u32[]{:S(2)}, u32[]{:S(2)}) %collective-permute-start.13) | collective-permute-done | bytes 98336 | tf_op jit(solution)/shard_map/ppermute | solution.py:45
  104.1 3.5 %collective-permute-done.12 = bf16[96,512]{1,0:T(8,128)(2,1)S(1)} collective-permute-done((bf16[96,512]{1,0:T(8,128)(2,1)S(1)}, bf16[96,512]{1,0:T(8,128)(2,1)S(1)}, u32[]{:S(2)}, u32[]{:S(2)}) %collective-permute-start.12) | collective-permute-done | bytes 98336 | tf_op jit(solution)/shard_map/ppermute | solution.py:45
  107.6 0.7 add_convert_fusion.1
  108.3 0.0 collective-permute-done.14
  108.3 0.2 slice_add_fusion
  108.5 1.0 fusion
  (1 shorter events, 0.0 us)
Async XLA Ops:
  3.4 20.8 %copy-start.2 = (bf16[96,896]{1,0:T(8,128)(2,1)S(1)}, bf16[96,896]{1,0:T(8,128)(2,1)}, u32[]{:S(2)}) copy-start(bf16[96,896]{1,0:T(8,128)(2,1)} %get-tuple-element.21) | copy-start | bytes 516100
  3.4 9.4 %collective-permute-start = (bf16[256,1024]{1,0:T(8,128)(2,1)}, bf16[256,1024]{1,0:T(8,128)(2,1)S(1)}, u32[]{:S(2)}, u32[]{:S(2)}) collective-permute-start(bf16[256,1024]{1,0:T(8,128)(2,1)} %get-tuple-element.22), channel_id=1, source_target_pairs={{0,1},{1,0},{2,3},{3,2},{4,5},{5,4},{6,7},{7,6},{8,9},{9,8},{10,11... | collective-permute-start | bytes 1572872 | tf_op jit(solution)/shard_map/ppermute | solution.py:45
  4.7 9.2 %collective-permute-start.1 = (bf16[96,896]{1,0:T(8,128)(2,1)}, bf16[96,896]{1,0:T(8,128)(2,1)S(1)}, u32[]{:S(2)}, u32[]{:S(2)}) collective-permute-start(bf16[96,896]{1,0:T(8,128)(2,1)} %get-tuple-element.21), channel_id=1, source_target_pairs={{0,4},{1,5},{2,6},{3,7},{4,0},{5,1},{6,2},{7,3},{8,12},{9,13},{10,... | collective-permute-start | bytes 516104 | tf_op jit(solution)/shard_map/ppermute | solution.py:45
  6.6 11.7 %collective-permute-start.3 = (bf16[96,896]{1,0:T(8,128)(2,1)}, bf16[96,896]{1,0:T(8,128)(2,1)S(1)}, u32[]{:S(2)}, u32[]{:S(2)}) collective-permute-start(bf16[96,896]{1,0:T(8,128)(2,1)} %get-tuple-element.21), channel_id=1, source_target_pairs={{0,12},{1,13},{2,14},{3,15},{4,8},{5,9},{6,10},{7,11},{8,4},{9,5},... | collective-permute-start | bytes 516104 | tf_op jit(solution)/shard_map/ppermute | solution.py:45
  9.4 14.7 %collective-permute-start.2 = (bf16[96,896]{1,0:T(8,128)(2,1)}, bf16[96,896]{1,0:T(8,128)(2,1)S(1)}, u32[]{:S(2)}, u32[]{:S(2)}) collective-permute-start(bf16[96,896]{1,0:T(8,128)(2,1)} %get-tuple-element.21), channel_id=1, source_target_pairs={{0,8},{1,9},{2,10},{3,11},{4,12},{5,13},{6,14},{7,15},{8,0},{9,1},... | collective-permute-start | bytes 516104 | tf_op jit(solution)/shard_map/ppermute | solution.py:45
  13.9 14.6 %copy-start = (bf16[512,1024]{1,0:T(8,128)(2,1)}, bf16[512,1024]{1,0:T(8,128)(2,1)S(1)}, u32[]{:S(2)}) copy-start(bf16[512,1024]{1,0:T(8,128)(2,1)S(1)} %pad_maximum_fusion.args_3_.args_5_) | copy-start | bytes 3145732
  13.9 25.0 %collective-permute-start.5 = (bf16[512,1024]{1,0:T(8,128)(2,1)S(1)}, bf16[512,1024]{1,0:T(8,128)(2,1)}, u32[]{:S(2)}, u32[]{:S(2)}) collective-permute-start(bf16[512,1024]{1,0:T(8,128)(2,1)S(1)} %pad_maximum_fusion.args_3_.args_5_), channel_id=1, source_target_pairs={{0,3},{1,2},{2,1},{3,0},{4,7},{5,6},{6,5},{7,4},{8,11},{9,10},{10,... | collective-permute-start | bytes 3145736 | tf_op jit(solution)/shard_map/ppermute | solution.py:45
  24.2 11.0 %collective-permute-start.4 = (bf16[384,896]{1,0:T(8,128)(2,1)S(1)}, bf16[384,896]{1,0:T(8,128)(2,1)S(1)}, u32[]{:S(2)}, u32[]{:S(2)}) collective-permute-start(bf16[384,896]{1,0:T(8,128)(2,1)S(1)} %pad_maximum_fusion.1), channel_id=1, source_target_pairs={{0,16},{1,17},{2,18},{3,19},{4,20},{5,21},{6,22},{7,23},{8,24},{9,... | collective-permute-start | bytes 2064392 | tf_op jit(solution)/shard_map/ppermute | solution.py:45
  36.2 20.9 %collective-permute-start.7 = (bf16[768,896]{1,0:T(8,128)(2,1)}, bf16[768,896]{1,0:T(8,128)(2,1)}, u32[]{:S(2)}, u32[]{:S(2)}) collective-permute-start(bf16[768,896]{1,0:T(8,128)(2,1)} %constant_dynamic-update-slice_fusion.args_0_.args_1_.args_2_), channel_id=1, source_target_pairs={{0,48},{1,49},{2,50},{3,51},{4,52},{5,53},{6,54},{7,55},{8,56},{9,... | collective-permute-start | bytes 4128776 | tf_op jit(solution)/shard_map/ppermute | solution.py:45
  56.6 19.6 %collective-permute-start.6 = (bf16[384,512]{1,0:T(8,128)(2,1)}, bf16[384,512]{1,0:T(8,128)(2,1)S(1)}, u32[]{:S(2)}, u32[]{:S(2)}) collective-permute-start(bf16[384,512]{1,0:T(8,128)(2,1)} %get-tuple-element.26), channel_id=1, source_target_pairs={{0,16},{1,17},{2,18},{3,19},{4,20},{5,21},{6,22},{7,23},{8,24},{9,... | collective-permute-start | bytes 1179656 | tf_op jit(solution)/shard_map/ppermute | solution.py:45
  57.1 37.9 %copy-start.3 = (bf16[384,512]{1,0:T(8,128)(2,1)S(1)}, bf16[384,512]{1,0:T(8,128)(2,1)}, u32[]{:S(2)}) copy-start(bf16[384,512]{1,0:T(8,128)(2,1)} %get-tuple-element.25) | copy-start | bytes 1179652
  76.1 19.1 %copy-start.1 = (bf16[512,1024]{1,0:T(8,128)(2,1)S(1)}, bf16[512,1024]{1,0:T(8,128)(2,1)}, u32[]{:S(2)}) copy-start(bf16[512,1024]{1,0:T(8,128)(2,1)} %get-tuple-element.35) | copy-start | bytes 3145732
  76.2 19.1 %collective-permute-start.10 = (bf16[512,1024]{1,0:T(8,128)(2,1)}, bf16[512,1024]{1,0:T(8,128)(2,1)S(1)}, u32[]{:S(2)}, u32[]{:S(2)}) collective-permute-start(bf16[512,1024]{1,0:T(8,128)(2,1)} %get-tuple-element.36), channel_id=1, source_target_pairs={{0,3},{1,2},{2,1},{3,0},{4,7},{5,6},{6,5},{7,4},{8,11},{9,10},{10,... | collective-permute-start | bytes 3145736 | tf_op jit(solution)/shard_map/ppermute | solution.py:45
  77.8 17.2 %collective-permute-start.8 = (bf16[384,512]{1,0:T(8,128)(2,1)}, bf16[384,512]{1,0:T(8,128)(2,1)S(1)}, u32[]{:S(2)}, u32[]{:S(2)}) collective-permute-start(bf16[384,512]{1,0:T(8,128)(2,1)} %get-tuple-element.33), channel_id=1, source_target_pairs={{0,48},{1,49},{2,50},{3,51},{4,52},{5,53},{6,54},{7,55},{8,56},{9,... | collective-permute-start | bytes 1179656 | tf_op jit(solution)/shard_map/ppermute | solution.py:45
  79.5 15.5 %collective-permute-start.9 = (bf16[384,512]{1,0:T(8,128)(2,1)}, bf16[384,512]{1,0:T(8,128)(2,1)S(1)}, u32[]{:S(2)}, u32[]{:S(2)}) collective-permute-start(bf16[384,512]{1,0:T(8,128)(2,1)} %get-tuple-element.34), channel_id=1, source_target_pairs={{0,32},{1,33},{2,34},{3,35},{4,36},{5,37},{6,38},{7,39},{8,40},{9,... | collective-permute-start | bytes 1179656 | tf_op jit(solution)/shard_map/ppermute | solution.py:45
  95.7 12.6 %collective-permute-start.14 = (bf16[256,1024]{1,0:T(8,128)(2,1)S(1)}, bf16[256,1024]{1,0:T(8,128)(2,1)S(1)}, u32[]{:S(2)}, u32[]{:S(2)}) collective-permute-start(bf16[256,1024]{1,0:T(8,128)(2,1)S(1)} %slice.40), channel_id=1, source_target_pairs={{0,1},{1,0},{2,3},{3,2},{4,5},{5,4},{6,7},{7,6},{8,9},{9,8},{10,11... | collective-permute-start | bytes 1572872 | tf_op jit(solution)/shard_map/ppermute | solution.py:45
  96.5 6.0 %collective-permute-start.11 = (bf16[96,512]{1,0:T(8,128)(2,1)S(1)}, bf16[96,512]{1,0:T(8,128)(2,1)S(1)}, u32[]{:S(2)}, u32[]{:S(2)}) collective-permute-start(bf16[96,512]{1,0:T(8,128)(2,1)S(1)} %get-tuple-element.41), channel_id=1, source_target_pairs={{0,4},{1,5},{2,6},{3,7},{4,0},{5,1},{6,2},{7,3},{8,12},{9,13},{10,... | collective-permute-start | bytes 294920 | tf_op jit(solution)/shard_map/ppermute | solution.py:45
  96.7 7.4 %collective-permute-start.13 = (bf16[96,512]{1,0:T(8,128)(2,1)S(1)}, bf16[96,512]{1,0:T(8,128)(2,1)S(1)}, u32[]{:S(2)}, u32[]{:S(2)}) collective-permute-start(bf16[96,512]{1,0:T(8,128)(2,1)S(1)} %get-tuple-element.42), channel_id=1, source_target_pairs={{0,12},{1,13},{2,14},{3,15},{4,8},{5,9},{6,10},{7,11},{8,4},{9,5},... | collective-permute-start | bytes 294920 | tf_op jit(solution)/shard_map/ppermute | solution.py:45
  99.5 8.1 %collective-permute-start.12 = (bf16[96,512]{1,0:T(8,128)(2,1)S(1)}, bf16[96,512]{1,0:T(8,128)(2,1)S(1)}, u32[]{:S(2)}, u32[]{:S(2)}) collective-permute-start(bf16[96,512]{1,0:T(8,128)(2,1)S(1)} %get-tuple-element.43), channel_id=1, source_target_pairs={{0,8},{1,9},{2,10},{3,11},{4,12},{5,13},{6,14},{7,15},{8,0},{9,1},... | collective-permute-start | bytes 294920 | tf_op jit(solution)/shard_map/ppermute | solution.py:45

commit v2 on v1

--- a/solution.py
+++ b/solution.py
@@ -47,9 +47,13 @@
 
 X_STEPS = ((1, 3), (3, 1))
 Y_STEPS = ((1, 3), (3, 1))
-Z_MASKS = (1, 2, 3)
+Z_MASKS = (2, 3, 1)
 PIECE = 384
 T_TILE = 256
+SHARD = 96
+GROUP = 32
+ROWS = 6 * SHARD + GROUP
+STATS = (NORM_PARTS + DELTA_PARTS) * HEADS
 
 
 def split_parts(value, count):
@@ -69,18 +73,24 @@
     for feature in range(HEADS * HALF):
         for part in range(DELTA_PARTS):
             head_sum[feature, (NORM_PARTS + part) * HEADS + feature // HALF] = 1
-    spread = np.zeros((LANES, HEADS // 2, LANES), np.float32)
-    for head in range(HEADS):
-        pair, odd = head // 2, head % 2
-        first = 0 if odd else HALF
-        for part in range(NORM_PARTS + DELTA_PARTS):
-            spread[part * HEADS + head, pair, first + part] = 1
-    return norm_place, head_sum, spread.reshape(LANES, HEADS // 2 * LANES)
+    groups = SHARD // GROUP
+    shift = np.zeros((groups, LANES, LANES), np.float32)
+    spread = np.zeros((LANES, HEADS // 2, groups, LANES), np.float32)
+    for group in range(groups):
+        for row in range(STATS):
+            shift[group, row, group * STATS + row] = 1
+        for head in range(HEADS):
+            pair, odd = head // 2, head % 2
+            first = 0 if odd else HALF
+            for part in range(NORM_PARTS + DELTA_PARTS):
+                row = group * STATS + part * HEADS + head
+                spread[row, pair, group, first + part] = 1
+    return norm_place, head_sum, shift, spread.reshape(LANES, HEADS // 2 * groups * LANES)
 
 
 def prologue_kernel(
-    queries, attn, w_out, truth, mask, log_norm, norm_place, head_sum, keys, values,
-    message, pack,
+    queries, attn, w_out, truth, mask, log_norm, norm_place, head_sum, shift,
+    keys, values, message, pack,
 ):
     pack[:, :512] = keys[...]
     pack[:, 512:] = values[...]
@@ -104,20 +114,26 @@
     deltas = jnp.where(
         lane < (NORM_PARTS + 1) * HEADS, delta_high.astype(F32), delta_low.astype(F32)
     )
-    message[:, :512] = queries[...]
-    message[:, 512:768] = residue
-    message[:, 768:] = (norms + deltas).astype(BF16)
-
-
-def attention_kernel(tiles, refs, carried, *args):
-    count = len(tiles)
+    stats = (norms + deltas).astype(BF16)
+    for pair in range(HEADS // 2):
+        message[pair * SHARD : (pair + 1) * SHARD, :] = queries[:, pair * LANES : (pair + 1) * LANES]
+    message[4 * SHARD : 5 * SHARD, :] = residue[:, :LANES]
+    message[5 * SHARD : 6 * SHARD, :] = residue[:, LANES:]
+    packed = sum(
+        dot(stats[at * GROUP : (at + 1) * GROUP], shift[at], NN) for at in range(shift.shape[0])
+    )
+    message[6 * SHARD :, :] = packed.astype(BF16)
+
+
+def attention_kernel(first_pair, shards, refs, carried, *args):
+    targets = shards * SHARD
     args = list(args)
     take = lambda n: [args.pop(0) for _ in range(n)]
-    q_refs, res_refs, st_refs = take(count), take(count), take(count)
+    (msg,) = take(1)
     k_refs, v_refs = take(len(refs)), take(len(refs))
     w_out, spread = take(2)
     sums_in = take(2) if carried else None
-    gq_outs = take(sum(tiles) // PIECE)
+    gq_outs = take(targets // PIECE)
     g_outs = take(len(refs)) if carried else take(2)
     qs, gs, ks, vs, gk_sum, gv_sum = args
     lane = lax.broadcasted_iota(jnp.int32, (1, LANES), 1)
@@ -128,17 +144,24 @@
     delta_lanes = jnp.where(
         place < NORM_PARTS, zero, jnp.where(place < NORM_PARTS + DELTA_PARTS, one, zero)
     )
-    start = 0
-    for size, q_ref, res_ref, st_ref in zip(tiles, q_refs, res_refs, st_refs):
-        rows = slice(start, start + size)
-        start += size
-        grads = dot(res_ref[...], w_out[...], NT).astype(BF16)
-        extra = dot(st_ref[...], spread[...], NN).astype(BF16)
-        query = q_ref[...]
+    gather = lambda at, size: jnp.concatenate(
+        [msg[m * ROWS + at : m * ROWS + at + size, :] for m in range(shards)], 0
+    )
+    residue = jnp.concatenate([gather(4 * SHARD, SHARD), gather(5 * SHARD, SHARD)], 1)
+    grads = dot(residue, w_out[...], NT).astype(BF16)
+    stats = gather(6 * SHARD, GROUP)
+    placed = dot(stats, spread[...], NN).astype(BF16)
+    groups = [placed[:, at * LANES : (at + 1) * LANES] for at in range(SHARD // GROUP)]
+    pair = pl.program_id(0) + first_pair
+    for m in range(shards):
+        rows = slice(m * SHARD, (m + 1) * SHARD)
+        query = msg[pl.ds(pl.multiple_of(m * ROWS + pair * SHARD, GROUP), SHARD), :]
+        extra = jnp.concatenate([g[m * GROUP : (m + 1) * GROUP] for g in groups], 0)
+        grad = grads[rows]
         qs[0, rows, :] = jnp.where(low, query, extra)
         qs[1, rows, :] = jnp.where(low, extra, query)
-        gs[0, rows, :] = jnp.where(low, grads, extra)
-        gs[1, rows, :] = jnp.where(low, extra, grads)
+        gs[0, rows, :] = jnp.where(low, grad, extra)
+        gs[1, rows, :] = jnp.where(low, extra, grad)
     start = 0
     for size, k_ref, v_ref in zip(refs, k_refs, v_refs):
         rows = slice(start, start + size)
@@ -149,7 +172,7 @@
         ks[1, rows, :] = jnp.where(low, norm_lanes, keys)
         vs[0, rows, :] = jnp.where(low, values, delta_lanes)
         vs[1, rows, :] = jnp.where(low, delta_lanes, values)
-    for first in range(0, sum(tiles), T_TILE):
+    for first in range(0, targets, T_TILE):
         rows = slice(first, first + T_TILE)
         gq = []
         for odd in range(2):
@@ -178,7 +201,6 @@
                 at - first : stop - first
             ]
             at = stop
-    here = pl.multiple_of(pl.program_id(0) * LANES, LANES)
     if not carried:
         g_outs[0][...] = gk_sum[...]
         g_outs[1][...] = gv_sum[...]
@@ -187,38 +209,36 @@
     for size, out in zip(refs, g_outs):
         cols = slice(start, start + size)
         start += size
-        out[:, pl.ds(here, LANES)] = (gk_sum[:, cols].T * 0.125).astype(BF16)
-        out[:, pl.ds(out.shape[1] // 2 + here, LANES)] = gv_sum[:, cols].T.astype(BF16)
-
-
-def attention(messages, packs, w_out, spread, first, pairs, sums=None):
+        out[:, :LANES] = (gk_sum[:, cols].T * 0.125).astype(BF16)
+        out[:, LANES:] = gv_sum[:, cols].T.astype(BF16)
+
+
+def attention(message, packs, w_out, spread, first, pairs, sums=None):
     carried = sums is not None
-    tiles = tuple(m.shape[0] for m in messages)
+    shards = message.shape[0] // ROWS
     refs = tuple(p.shape[0] for p in packs)
-    targets, total = sum(tiles), sum(refs)
+    targets, total = shards * SHARD, sum(refs)
     spec = pl.BlockSpec
-    in_specs = [spec((t, LANES), lambda j: (0, first + j)) for t in tiles]
-    in_specs += [spec((t, 256), lambda j: (0, 2)) for t in tiles]
-    in_specs += [spec((t, LANES), lambda j: (0, 6)) for t in tiles]
+    in_specs = [spec(message.shape, lambda j: (0, 0))]
     in_specs += [spec((r, LANES), lambda j: (0, first + j)) for r in refs]
     in_specs += [spec((r, LANES), lambda j: (0, 4 + first + j)) for r in refs]
     in_specs += [
         spec((LANES, 256), lambda j: (first + j, 0)),
-        spec((LANES, LANES), lambda j: (0, first + j)),
+        spec((LANES, SHARD // GROUP * LANES), lambda j: (0, first + j)),
     ]
-    operands = list(messages) * 3 + list(packs) * 2 + [w_out, spread]
+    operands = [message] + list(packs) * 2 + [w_out, spread]
     out_specs = [spec((PIECE, LANES), lambda j: (0, j))] * (targets // PIECE)
     out_shape = [jax.ShapeDtypeStruct((PIECE, pairs * LANES), BF16)] * (targets // PIECE)
     if carried:
         in_specs += [spec((LANES, total), lambda j: (first + j, 0))] * 2
         operands += list(sums)
-        out_specs += [spec((r, 2 * LANES * pairs), lambda j: (0, 0)) for r in refs]
+        out_specs += [spec((r, 2 * LANES), lambda j: (0, j)) for r in refs]
         out_shape += [jax.ShapeDtypeStruct((r, 2 * LANES * pairs), BF16) for r in refs]
     else:
         out_specs += [spec((LANES, total), lambda j: (j, 0))] * 2
         out_shape += [jax.ShapeDtypeStruct((LANES * pairs, total), F32)] * 2
     return pl.pallas_call(
-        functools.partial(attention_kernel, tiles, refs, carried),
+        functools.partial(attention_kernel, first, shards, refs, carried),
         grid=(pairs,),
         in_specs=in_specs,
         out_specs=out_specs,
@@ -238,26 +258,34 @@
     )(*operands)
 
 
+def split_kernel(near, other, keys_out, values_out):
+    total = near[...] + other[...].astype(F32)
+    for pair in range(HEADS // 2):
+        lanes = slice(pair * LANES, (pair + 1) * LANES)
+        keys_out[:, lanes] = total[:, 2 * pair * LANES : (2 * pair + 1) * LANES]
+        values_out[:, lanes] = total[:, (2 * pair + 1) * LANES : (2 * pair + 2) * LANES]
+
+
 def total_of(parts):
     return sum(part.astype(F32) for part in parts).astype(BF16)
 
 
 def body(queries, ref_keys, ref_values, attn_out, log_norm, w_out, dosage_truth, marker_mask):
-    norm_place, head_sum, spread = (jnp.asarray(m, BF16) for m in place_matrices())
+    norm_place, head_sum, shift, spread = (jnp.asarray(m, BF16) for m in place_matrices())
     message, pack = pl.pallas_call(
         prologue_kernel,
         out_shape=[
-            jax.ShapeDtypeStruct((queries.shape[0], 896), BF16),
+            jax.ShapeDtypeStruct((ROWS, LANES), BF16),
             jax.ShapeDtypeStruct((ref_keys.shape[0], 1024), BF16),
         ],
         compiler_params=pltpu.CompilerParams(vmem_limit_bytes=62 * 2**20),
     )(
         queries, attn_out, w_out, dosage_truth, marker_mask[None, :], log_norm,
-        norm_place, head_sum, ref_keys, ref_values,
+        norm_place, head_sum, shift, ref_keys, ref_values,
     )
     pack = jnp.concatenate([pack, exchange(pack, "y", Y_STEPS[0])], 0)
     along = [exchange(message, "z", (m, m)) for m in Z_MASKS]
-    pack, along[0] = lax.optimization_barrier((pack, along[0]))
+    pack, along[2] = lax.optimization_barrier((pack, along[2]))
     message = jnp.concatenate([message] + along, 0)
     pack_far = exchange(pack, "y", Y_STEPS[1])
     beside = exchange(message, "x", X_STEPS[0])
@@ -265,9 +293,9 @@
     far = exchange(both, "x", X_STEPS[1])
     packs = [pack, pack_far]
 
-    gq_mine, gq_beside, *sums = attention([both], packs, w_out, spread, 0, 4)
+    gq_mine, gq_beside, *sums = attention(both, packs, w_out, spread, 0, 4)
     back = exchange(gq_beside, "x", X_STEPS[0])
-    gq_near, gq_far, near_kv, far_kv = attention([far], packs, w_out, spread, 0, 4, sums)
+    gq_near, gq_far, near_kv, far_kv = attention(far, packs, w_out, spread, 0, 4, sums)
     back, gq_near, gq_far, far_kv = lax.optimization_barrier((back, gq_near, gq_far, far_kv))
     got_kv = exchange(far_kv, "y", Y_STEPS[1])
     across = exchange(gq_far, "x", (2, 2))
@@ -284,8 +312,12 @@
         [part(0)]
         + [exchange(part(at + 1), "z", (m, m)) for at, m in enumerate(Z_MASKS)]
     )
-    total = half_kv[:refs_here] + exchange(other, "y", Y_STEPS[0]).astype(F32)
-    return grad_query, total[:, :512], total[:, 512:]
+    grad_keys, grad_values = pl.pallas_call(
+        split_kernel,
+        out_shape=[jax.ShapeDtypeStruct((refs_here, 512), F32)] * 2,
+        compiler_params=pltpu.CompilerParams(vmem_limit_bytes=32 * 2**20),
+    )(half_kv[:refs_here], exchange(other, "y", Y_STEPS[0]))
+    return grad_query, grad_keys, grad_values
 
 
 def solution(mesh):

time: 110 us -> 107 us (0.973)
  waiting for transfers between devices: 40 us -> 36 us
  Pallas kernels: 39.4 us -> 40.5 us
    ppermute x15, waiting for transfers between devices: 40 us -> 36 us  [exchange(): return lax.ppermute(array, AXES, pairs)]
    pallas_call x3 -> x4, Pallas kernels: 39.4 us -> 40.5 us  [the longest x2 36.5 us: attention(): pl.pallas_call(functools.partial(attention_kernel, first, shards, refs, c...]
  transfers between devices with their start and end apart: 15 -> 15, of which waited for: 8 -> 7; matrix products, arithmetic and copies ran while one was open for 5% -> 5% of each run, Pallas kernels for 33% -> 34%
where the time goes in v2:
time: 107 us; the launch traced here: 106 us
  Pallas kernels  40.5 us (38%)
  waiting for transfers between devices  36 us (34%)
  starting transfers between devices  22.7 us (21%)
  local copies, waits for them, and re-layouts  3.76 us (4%)
  other arithmetic  2.43 us (2%)
    pallas_call x2, Pallas kernels, attention(): pl.pallas_call(functools.partial(attention_kernel, first, shards, refs, c...  36.5 us
    ppermute x15, waiting for transfers between devices, exchange(): return lax.ppermute(array, AXES, pairs)  36 us
    ppermute x15, starting transfers between devices, exchange(): return lax.ppermute(array, AXES, pairs)  22.7 us
    pallas_call x1, Pallas kernels, body(): pl.pallas_call(prologue_kernel, out_shape=[jax.ShapeDtypeStruct((ROWS, LA...  2.87 us
    unnamed x12, local copies, waits for them, and re-layouts  2.72 us
  transfers between devices with their start and end apart: 15, of which 7 were waited for; matrix products, arithmetic and copies ran while one was open for 5% of the time, Pallas kernels for 34%

profile of v2, /device:TPU:16, one launch (start us, length us, event | category | flops | bytes accessed | tf_op | source)
XLA Modules:
  0.0 106.2 jit_solution(17401119184776940108)
XLA Ops:
  0.6 2.9 %shard_map.139 = (bf16[608,128]{1,0:T(8,128)(2,1)}, bf16[256,1024]{1,0:T(8,128)(2,1)}) custom-call(bf16[96,512]{1,0:T(8,128)(2,1)} %queries.1, bf16[96,512]{1,0:T(8,128)(2,1)} %attn.1, bf16[512,256]{1,0:T(8,128)(2,1)} %args_5_.6, f32[96,256]{1,0:T(8,128)} %truth.1, s32[1,256]{1,0:T(1,128)} %bitcast.1, f32[8,96]{1,0:T(8,128)} %log_norm.1, ...), custom_call_target="tpu_custom_call" | custom-call | tf_op jit(solution)/shard_map/pallas_call | solution.py:275
  3.5 0.0 copy-start.2
  3.5 1.3 %collective-permute-start.2 = (bf16[256,1024]{1,0:T(8,128)(2,1)}, bf16[256,1024]{1,0:T(8,128)(2,1)S(1)}, u32[]{:S(2)}, u32[]{:S(2)}) collective-permute-start(bf16[256,1024]{1,0:T(8,128)(2,1)} %get-tuple-element.24), channel_id=1, source_target_pairs={{0,1},{1,0},{2,3},{3,2},{4,5},{5,4},{6,7},{7,6},{8,9},{9,8},{10,11... | collective-permute-start | bytes 1572872 | tf_op jit(solution)/shard_map/ppermute | solution.py:45
  4.8 1.9 %collective-permute-start.3 = (bf16[608,128]{1,0:T(8,128)(2,1)}, bf16[608,128]{1,0:T(8,128)(2,1)S(1)}, u32[]{:S(2)}, u32[]{:S(2)}) collective-permute-start(bf16[608,128]{1,0:T(8,128)(2,1)} %get-tuple-element.23), channel_id=1, source_target_pairs={{0,4},{1,5},{2,6},{3,7},{4,0},{5,1},{6,2},{7,3},{8,12},{9,13},{10,... | collective-permute-start | bytes 466952 | tf_op jit(solution)/shard_map/ppermute | solution.py:45
  6.7 2.8 %collective-permute-start.1 = (bf16[608,128]{1,0:T(8,128)(2,1)}, bf16[608,128]{1,0:T(8,128)(2,1)S(1)}, u32[]{:S(2)}, u32[]{:S(2)}) collective-permute-start(bf16[608,128]{1,0:T(8,128)(2,1)} %get-tuple-element.23), channel_id=1, source_target_pairs={{0,12},{1,13},{2,14},{3,15},{4,8},{5,9},{6,10},{7,11},{8,4},{9,5},... | collective-permute-start | bytes 466952 | tf_op jit(solution)/shard_map/ppermute | solution.py:45
  9.5 0.5 collective-permute-start
  10.0 2.9 %collective-permute-done.2 = bf16[256,1024]{1,0:T(8,128)(2,1)S(1)} collective-permute-done((bf16[256,1024]{1,0:T(8,128)(2,1)}, bf16[256,1024]{1,0:T(8,128)(2,1)S(1)}, u32[]{:S(2)}, u32[]{:S(2)}) %collective-permute-start.2) | collective-permute-done | bytes 524320 | tf_op jit(solution)/shard_map/ppermute | solution.py:45
  12.9 1.1 %pad_maximum_fusion.args_1_.args_3_ = bf16[512,1024]{1,0:T(8,128)(2,1)S(1)} fusion(bf16[256,1024]{1,0:T(8,128)(2,1)S(1)} %collective-permute-done.2, bf16[256,1024]{1,0:T(8,128)(2,1)} %get-tuple-element.24), kind=kLoop, calls=%fused_computation.2 | loop fusion | flops 2097152 | bytes 2097152 | tf_op jit(solution)/shard_map/concatenate | solution.py:286
  14.0 0.0 copy-start
  14.0 0.0 collective-permute-done.3
  14.0 0.7 collective-permute-start.5
  14.7 2.8 %collective-permute-done.1 = bf16[608,128]{1,0:T(8,128)(2,1)S(1)} collective-permute-done((bf16[608,128]{1,0:T(8,128)(2,1)}, bf16[608,128]{1,0:T(8,128)(2,1)S(1)}, u32[]{:S(2)}, u32[]{:S(2)}) %collective-permute-start.1) | collective-permute-done | bytes 155680 | tf_op jit(solution)/shard_map/ppermute | solution.py:45
  17.5 5.3 %collective-permute-done = bf16[608,128]{1,0:T(8,128)(2,1)S(1)} collective-permute-done((bf16[608,128]{1,0:T(8,128)(2,1)}, bf16[608,128]{1,0:T(8,128)(2,1)S(1)}, u32[]{:S(2)}, u32[]{:S(2)}) %collective-permute-start) | collective-permute-done | bytes 155680 | tf_op jit(solution)/shard_map/ppermute | solution.py:45
  22.9 0.0 copy-done.2
  22.9 1.6 %collective-permute-start.4 = (bf16[2432,128]{1,0:T(8,128)(2,1)S(1)}, bf16[2432,128]{1,0:T(8,128)(2,1)S(1)}, u32[]{:S(2)}, u32[]{:S(2)}) collective-permute-start(bf16[2432,128]{1,0:T(8,128)(2,1)S(1)} %pad_maximum_fusion.1), channel_id=1, source_target_pairs={{0,16},{1,17},{2,18},{3,19},{4,20},{5,21},{6,22},{7,23},{8,24},{9,... | collective-permute-start | bytes 1867784 | tf_op jit(solution)/shard_map/ppermute | solution.py:45
  24.5 0.7 constant_dynamic-update-slice_fusion.4
  25.2 0.7 constant_dynamic-update-slice_fusion.3
  25.8 0.7 constant_dynamic-update-slice_fusion.2
  26.5 0.7 constant_dynamic-update-slice_fusion.1
  27.2 0.0 copy-done
  27.2 6.0 %collective-permute-done.4 = bf16[2432,128]{1,0:T(8,128)(2,1)S(1)} collective-permute-done((bf16[2432,128]{1,0:T(8,128)(2,1)S(1)}, bf16[2432,128]{1,0:T(8,128)(2,1)S(1)}, u32[]{:S(2)}, u32[]{:S(2)}) %collective-permute-start.4) | collective-permute-done | bytes 622624 | tf_op jit(solution)/shard_map/ppermute | solution.py:45
  33.2 0.9 constant_dynamic-update-slice_fusion.args_0_
  34.1 2.8 %collective-permute-start.7 = (bf16[4864,128]{1,0:T(8,128)(2,1)}, bf16[4864,128]{1,0:T(8,128)(2,1)}, u32[]{:S(2)}, u32[]{:S(2)}) collective-permute-start(bf16[4864,128]{1,0:T(8,128)(2,1)} %constant_dynamic-update-slice_fusion.args_0_), channel_id=1, source_target_pairs={{0,48},{1,49},{2,50},{3,51},{4,52},{5,53},{6,54},{7,55},{8,56},{9,... | collective-permute-start | bytes 3735560 | tf_op jit(solution)/shard_map/ppermute | solution.py:45
  36.9 0.0 collective-permute-done.5.args_2_.args_4_
  36.9 17.9 %shard_map.140 = (bf16[384,512]{1,0:T(8,128)(2,1)}, bf16[384,512]{1,0:T(8,128)(2,1)}, f32[512,1024]{1,0:T(8,128)}, f32[512,1024]{1,0:T(8,128)}) custom-call(bf16[4864,128]{1,0:T(8,128)(2,1)} %constant_dynamic-update-slice_fusion.args_0_, bf16[512,1024]{1,0:T(8,128)(2,1)} %copy-done, bf16[512,1024]{1,0:T(8,128)(2,1)} %collective-permute-done.5.args_2_.args_4_, ...), custom_call_target="tpu_custom_call" | custom-call | flops 16106127360 | bytes 4194304 | tf_op jit(solution)/shard_map/pallas_call | solution.py:240
  54.8 0.4 collective-permute-start.6
  55.2 0.0 collective-permute-done.7.args_0_
  55.3 0.0 copy-start.3
  55.3 18.6 %shard_map.141 = (bf16[384,512]{1,0:T(8,128)(2,1)}, bf16[384,512]{1,0:T(8,128)(2,1)}, bf16[512,1024]{1,0:T(8,128)(2,1)}, bf16[512,1024]{1,0:T(8,128)(2,1)}) custom-call(bf16[4864,128]{1,0:T(8,128)(2,1)} %collective-permute-done.7.args_0_, bf16[512,1024]{1,0:T(8,128)(2,1)} %copy-done, bf16[512,1024]{1,0:T(8,128)(2,1)} %collective-permute-done.5.args_2_.args_4_, ...), custom_call_target="tpu_custom_call" | custom-call | flops 16106127360 | bytes 4194304 | tf_op jit(solution)/shard_map/pallas_call | solution.py:240
  73.9 0.0 copy-start.1
  73.9 0.0 collective-permute-done.6
  73.9 1.7 %collective-permute-start.10 = (bf16[512,1024]{1,0:T(8,128)(2,1)}, bf16[512,1024]{1,0:T(8,128)(2,1)S(1)}, u32[]{:S(2)}, u32[]{:S(2)}) collective-permute-start(bf16[512,1024]{1,0:T(8,128)(2,1)} %get-tuple-element.38), channel_id=1, source_target_pairs={{0,3},{1,2},{2,1},{3,0},{4,7},{5,6},{6,5},{7,4},{8,11},{9,10},{10,... | collective-permute-start | bytes 3145736 | tf_op jit(solution)/shard_map/ppermute | solution.py:45
  75.6 1.1 %collective-permute-start.8 = (bf16[384,512]{1,0:T(8,128)(2,1)}, bf16[384,512]{1,0:T(8,128)(2,1)S(1)}, u32[]{:S(2)}, u32[]{:S(2)}) collective-permute-start(bf16[384,512]{1,0:T(8,128)(2,1)} %get-tuple-element.35), channel_id=1, source_target_pairs={{0,48},{1,49},{2,50},{3,51},{4,52},{5,53},{6,54},{7,55},{8,56},{9,... | collective-permute-start | bytes 1179656 | tf_op jit(solution)/shard_map/ppermute | solution.py:45
  76.7 2.7 %collective-permute-start.9 = (bf16[384,512]{1,0:T(8,128)(2,1)}, bf16[384,512]{1,0:T(8,128)(2,1)S(1)}, u32[]{:S(2)}, u32[]{:S(2)}) collective-permute-start(bf16[384,512]{1,0:T(8,128)(2,1)} %get-tuple-element.36), channel_id=1, source_target_pairs={{0,32},{1,33},{2,34},{3,35},{4,36},{5,37},{6,38},{7,39},{8,40},{9,... | collective-permute-start | bytes 1179656 | tf_op jit(solution)/shard_map/ppermute | solution.py:45
  79.4 13.5 %collective-permute-done.8 = bf16[384,512]{1,0:T(8,128)(2,1)S(1)} collective-permute-done((bf16[384,512]{1,0:T(8,128)(2,1)}, bf16[384,512]{1,0:T(8,128)(2,1)S(1)}, u32[]{:S(2)}, u32[]{:S(2)}) %collective-permute-start.8) | collective-permute-done | bytes 393248 | tf_op jit(solution)/shard_map/ppermute | solution.py:45
  93.0 0.0 collective-permute-done.9
  93.0 0.0 copy-done.3
  93.0 0.2 add_convert_fusion
  93.2 0.0 collective-permute-done.10
  93.2 0.0 copy-done.1
  93.2 0.4 convert_add_fusion
  93.6 0.1 slice.29
  93.7 0.8 collective-permute-start.14
  94.4 0.1 collective-permute-start.11
  94.5 3.3 %collective-permute-start.13 = (bf16[96,512]{1,0:T(8,128)(2,1)S(1)}, bf16[96,512]{1,0:T(8,128)(2,1)S(1)}, u32[]{:S(2)}, u32[]{:S(2)}) collective-permute-start(bf16[96,512]{1,0:T(8,128)(2,1)S(1)} %get-tuple-element.44), channel_id=1, source_target_pairs={{0,4},{1,5},{2,6},{3,7},{4,0},{5,1},{6,2},{7,3},{8,12},{9,13},{10,... | collective-permute-start | bytes 294920 | tf_op jit(solution)/shard_map/ppermute | solution.py:45
  97.8 1.1 %collective-permute-start.12 = (bf16[96,512]{1,0:T(8,128)(2,1)S(1)}, bf16[96,512]{1,0:T(8,128)(2,1)S(1)}, u32[]{:S(2)}, u32[]{:S(2)}) collective-permute-start(bf16[96,512]{1,0:T(8,128)(2,1)S(1)} %get-tuple-element.45), channel_id=1, source_target_pairs={{0,12},{1,13},{2,14},{3,15},{4,8},{5,9},{6,10},{7,11},{8,4},{9,5},... | collective-permute-start | bytes 294920 | tf_op jit(solution)/shard_map/ppermute | solution.py:45
  98.9 0.1 slice.26.near
  99.0 3.7 %collective-permute-done.11 = bf16[96,512]{1,0:T(8,128)(2,1)S(1)} collective-permute-done((bf16[96,512]{1,0:T(8,128)(2,1)S(1)}, bf16[96,512]{1,0:T(8,128)(2,1)S(1)}, u32[]{:S(2)}, u32[]{:S(2)}) %collective-permute-start.11) | collective-permute-done | bytes 98336 | tf_op jit(solution)/shard_map/ppermute | solution.py:45
  102.7 0.0 collective-permute-done.13
  102.7 1.6 %collective-permute-done.12 = bf16[96,512]{1,0:T(8,128)(2,1)S(1)} collective-permute-done((bf16[96,512]{1,0:T(8,128)(2,1)S(1)}, bf16[96,512]{1,0:T(8,128)(2,1)S(1)}, u32[]{:S(2)}, u32[]{:S(2)}) %collective-permute-start.12) | collective-permute-done | bytes 98336 | tf_op jit(solution)/shard_map/ppermute | solution.py:45
  104.3 0.7 add_convert_fusion.1
  105.0 0.0 collective-permute-done.14.other
  105.0 1.1 %shard_map.142 = (f32[256,512]{1,0:T(8,128)}, f32[256,512]{1,0:T(8,128)}) custom-call(f32[256,1024]{1,0:T(8,128)S(1)} %slice.26.near, bf16[256,1024]{1,0:T(8,128)(2,1)S(1)} %collective-permute-done.14.other), custom_call_target="tpu_custom_call" | custom-call | tf_op jit(solution)/shard_map/pallas_call | solution.py:315
  (2 shorter events, 0.1 us)
Async XLA Ops:
  3.5 19.4 %copy-start.2 = (bf16[608,128]{1,0:T(8,128)(2,1)S(1)}, bf16[608,128]{1,0:T(8,128)(2,1)}, u32[]{:S(2)}) copy-start(bf16[608,128]{1,0:T(8,128)(2,1)} %get-tuple-element.23) | copy-start | bytes 466948
  3.5 9.4 %collective-permute-start.2 = (bf16[256,1024]{1,0:T(8,128)(2,1)}, bf16[256,1024]{1,0:T(8,128)(2,1)S(1)}, u32[]{:S(2)}, u32[]{:S(2)}) collective-permute-start(bf16[256,1024]{1,0:T(8,128)(2,1)} %get-tuple-element.24), channel_id=1, source_target_pairs={{0,1},{1,0},{2,3},{3,2},{4,5},{5,4},{6,7},{7,6},{8,9},{9,8},{10,11... | collective-permute-start | bytes 1572872 | tf_op jit(solution)/shard_map/ppermute | solution.py:45
  4.8 9.2 %collective-permute-start.3 = (bf16[608,128]{1,0:T(8,128)(2,1)}, bf16[608,128]{1,0:T(8,128)(2,1)S(1)}, u32[]{:S(2)}, u32[]{:S(2)}) collective-permute-start(bf16[608,128]{1,0:T(8,128)(2,1)} %get-tuple-element.23), channel_id=1, source_target_pairs={{0,4},{1,5},{2,6},{3,7},{4,0},{5,1},{6,2},{7,3},{8,12},{9,13},{10,... | collective-permute-start | bytes 466952 | tf_op jit(solution)/shard_map/ppermute | solution.py:45
  6.7 10.8 %collective-permute-start.1 = (bf16[608,128]{1,0:T(8,128)(2,1)}, bf16[608,128]{1,0:T(8,128)(2,1)S(1)}, u32[]{:S(2)}, u32[]{:S(2)}) collective-permute-start(bf16[608,128]{1,0:T(8,128)(2,1)} %get-tuple-element.23), channel_id=1, source_target_pairs={{0,12},{1,13},{2,14},{3,15},{4,8},{5,9},{6,10},{7,11},{8,4},{9,5},... | collective-permute-start | bytes 466952 | tf_op jit(solution)/shard_map/ppermute | solution.py:45
  9.5 13.3 %collective-permute-start = (bf16[608,128]{1,0:T(8,128)(2,1)}, bf16[608,128]{1,0:T(8,128)(2,1)S(1)}, u32[]{:S(2)}, u32[]{:S(2)}) collective-permute-start(bf16[608,128]{1,0:T(8,128)(2,1)} %get-tuple-element.23), channel_id=1, source_target_pairs={{0,8},{1,9},{2,10},{3,11},{4,12},{5,13},{6,14},{7,15},{8,0},{9,1},... | collective-permute-start | bytes 466952 | tf_op jit(solution)/shard_map/ppermute | solution.py:45
  14.0 13.2 %copy-start = (bf16[512,1024]{1,0:T(8,128)(2,1)}, bf16[512,1024]{1,0:T(8,128)(2,1)S(1)}, u32[]{:S(2)}) copy-start(bf16[512,1024]{1,0:T(8,128)(2,1)S(1)} %pad_maximum_fusion.args_1_.args_3_) | copy-start | bytes 3145732
  14.0 22.8 %collective-permute-start.5 = (bf16[512,1024]{1,0:T(8,128)(2,1)S(1)}, bf16[512,1024]{1,0:T(8,128)(2,1)}, u32[]{:S(2)}, u32[]{:S(2)}) collective-permute-start(bf16[512,1024]{1,0:T(8,128)(2,1)S(1)} %pad_maximum_fusion.args_1_.args_3_), channel_id=1, source_target_pairs={{0,3},{1,2},{2,1},{3,0},{4,7},{5,6},{6,5},{7,4},{8,11},{9,10},{10,... | collective-permute-start | bytes 3145736 | tf_op jit(solution)/shard_map/ppermute | solution.py:45
  22.9 10.3 %collective-permute-start.4 = (bf16[2432,128]{1,0:T(8,128)(2,1)S(1)}, bf16[2432,128]{1,0:T(8,128)(2,1)S(1)}, u32[]{:S(2)}, u32[]{:S(2)}) collective-permute-start(bf16[2432,128]{1,0:T(8,128)(2,1)S(1)} %pad_maximum_fusion.1), channel_id=1, source_target_pairs={{0,16},{1,17},{2,18},{3,19},{4,20},{5,21},{6,22},{7,23},{8,24},{9,... | collective-permute-start | bytes 1867784 | tf_op jit(solution)/shard_map/ppermute | solution.py:45
  34.1 21.1 %collective-permute-start.7 = (bf16[4864,128]{1,0:T(8,128)(2,1)}, bf16[4864,128]{1,0:T(8,128)(2,1)}, u32[]{:S(2)}, u32[]{:S(2)}) collective-permute-start(bf16[4864,128]{1,0:T(8,128)(2,1)} %constant_dynamic-update-slice_fusion.args_0_), channel_id=1, source_target_pairs={{0,48},{1,49},{2,50},{3,51},{4,52},{5,53},{6,54},{7,55},{8,56},{9,... | collective-permute-start | bytes 3735560 | tf_op jit(solution)/shard_map/ppermute | solution.py:45
  54.8 19.1 %collective-permute-start.6 = (bf16[384,512]{1,0:T(8,128)(2,1)}, bf16[384,512]{1,0:T(8,128)(2,1)S(1)}, u32[]{:S(2)}, u32[]{:S(2)}) collective-permute-start(bf16[384,512]{1,0:T(8,128)(2,1)} %get-tuple-element.28), channel_id=1, source_target_pairs={{0,16},{1,17},{2,18},{3,19},{4,20},{5,21},{6,22},{7,23},{8,24},{9,... | collective-permute-start | bytes 1179656 | tf_op jit(solution)/shard_map/ppermute | solution.py:45
  55.3 37.7 %copy-start.3 = (bf16[384,512]{1,0:T(8,128)(2,1)S(1)}, bf16[384,512]{1,0:T(8,128)(2,1)}, u32[]{:S(2)}) copy-start(bf16[384,512]{1,0:T(8,128)(2,1)} %get-tuple-element.27) | copy-start | bytes 1179652
  73.9 19.3 %copy-start.1 = (bf16[512,1024]{1,0:T(8,128)(2,1)S(1)}, bf16[512,1024]{1,0:T(8,128)(2,1)}, u32[]{:S(2)}) copy-start(bf16[512,1024]{1,0:T(8,128)(2,1)} %get-tuple-element.37) | copy-start | bytes 3145732
  73.9 19.3 %collective-permute-start.10 = (bf16[512,1024]{1,0:T(8,128)(2,1)}, bf16[512,1024]{1,0:T(8,128)(2,1)S(1)}, u32[]{:S(2)}, u32[]{:S(2)}) collective-permute-start(bf16[512,1024]{1,0:T(8,128)(2,1)} %get-tuple-element.38), channel_id=1, source_target_pairs={{0,3},{1,2},{2,1},{3,0},{4,7},{5,6},{6,5},{7,4},{8,11},{9,10},{10,... | collective-permute-start | bytes 3145736 | tf_op jit(solution)/shard_map/ppermute | solution.py:45
  75.6 17.4 %collective-permute-start.8 = (bf16[384,512]{1,0:T(8,128)(2,1)}, bf16[384,512]{1,0:T(8,128)(2,1)S(1)}, u32[]{:S(2)}, u32[]{:S(2)}) collective-permute-start(bf16[384,512]{1,0:T(8,128)(2,1)} %get-tuple-element.35), channel_id=1, source_target_pairs={{0,48},{1,49},{2,50},{3,51},{4,52},{5,53},{6,54},{7,55},{8,56},{9,... | collective-permute-start | bytes 1179656 | tf_op jit(solution)/shard_map/ppermute | solution.py:45
  76.7 16.3 %collective-permute-start.9 = (bf16[384,512]{1,0:T(8,128)(2,1)}, bf16[384,512]{1,0:T(8,128)(2,1)S(1)}, u32[]{:S(2)}, u32[]{:S(2)}) collective-permute-start(bf16[384,512]{1,0:T(8,128)(2,1)} %get-tuple-element.36), channel_id=1, source_target_pairs={{0,32},{1,33},{2,34},{3,35},{4,36},{5,37},{6,38},{7,39},{8,40},{9,... | collective-permute-start | bytes 1179656 | tf_op jit(solution)/shard_map/ppermute | solution.py:45
  93.7 11.4 %collective-permute-start.14 = (bf16[256,1024]{1,0:T(8,128)(2,1)S(1)}, bf16[256,1024]{1,0:T(8,128)(2,1)S(1)}, u32[]{:S(2)}, u32[]{:S(2)}) collective-permute-start(bf16[256,1024]{1,0:T(8,128)(2,1)S(1)} %slice.29), channel_id=1, source_target_pairs={{0,1},{1,0},{2,3},{3,2},{4,5},{5,4},{6,7},{7,6},{8,9},{9,8},{10,11... | collective-permute-start | bytes 1572872 | tf_op jit(solution)/shard_map/ppermute | solution.py:45
  94.4 8.3 %collective-permute-start.11 = (bf16[96,512]{1,0:T(8,128)(2,1)S(1)}, bf16[96,512]{1,0:T(8,128)(2,1)S(1)}, u32[]{:S(2)}, u32[]{:S(2)}) collective-permute-start(bf16[96,512]{1,0:T(8,128)(2,1)S(1)} %get-tuple-element.43), channel_id=1, source_target_pairs={{0,8},{1,9},{2,10},{3,11},{4,12},{5,13},{6,14},{7,15},{8,0},{9,1},... | collective-permute-start | bytes 294920 | tf_op jit(solution)/shard_map/ppermute | solution.py:45
  94.5 8.2 %collective-permute-start.13 = (bf16[96,512]{1,0:T(8,128)(2,1)S(1)}, bf16[96,512]{1,0:T(8,128)(2,1)S(1)}, u32[]{:S(2)}, u32[]{:S(2)}) collective-permute-start(bf16[96,512]{1,0:T(8,128)(2,1)S(1)} %get-tuple-element.44), channel_id=1, source_target_pairs={{0,4},{1,5},{2,6},{3,7},{4,0},{5,1},{6,2},{7,3},{8,12},{9,13},{10,... | collective-permute-start | bytes 294920 | tf_op jit(solution)/shard_map/ppermute | solution.py:45
  97.8 6.5 %collective-permute-start.12 = (bf16[96,512]{1,0:T(8,128)(2,1)S(1)}, bf16[96,512]{1,0:T(8,128)(2,1)S(1)}, u32[]{:S(2)}, u32[]{:S(2)}) collective-permute-start(bf16[96,512]{1,0:T(8,128)(2,1)S(1)} %get-tuple-element.45), channel_id=1, source_target_pairs={{0,12},{1,13},{2,14},{3,15},{4,8},{5,9},{6,10},{7,11},{8,4},{9,5},... | collective-permute-start | bytes 294920 | tf_op jit(solution)/shard_map/ppermute | solution.py:45
